TPU v7x, 256 devices: a whole 4x4x8 slice. The times are simulated.
256 devices in a mesh: tile: 16 (over z, x_hi), slab: 16 (over x_lo, y, core).
Axes of the slice: x: 4 (x_hi: 2, x_lo: 2; x = x_hi * 2 + x_lo), y: 4, z: 8, core: 2. Of those that a mesh axis runs over, the one named last changes fastest.
Arguments:
- start_volt: float32 [2, 128, 512, 2048], P(None, 'slab', 'tile'), may hold values from -6 to 6
- cap_rate: float32 [2, 512, 2048], P(None, 'tile'), may hold values from 0.2 to 0.6
- horiz_cond: float32 [2, 512, 2048], P(None, 'tile'), may hold values from 0.6 to 1.8
- vert_cond: float32 [2, 512, 2048], P(None, 'tile'), may hold values from 0.2 to 0.6
- via_cond: float32 [512, 2048], P('tile'), may hold values from 0.3 to 1
- line_inverse: float32 [2, 16, 128, 128], replicated, may hold values from 0 to 0.5
- cell_node: int32 [32768], P('tile'), may hold values from 0 to 65535
- cell_phase: int32 [32768], P('tile'), may hold values from 0 to 127
- cell_amp: float32 [32768], P('tile'), may hold values from 0.5 to 4
Outputs:
- voltage: float32 [2, 128, 512, 2048], P(None, 'slab', 'tile')
Inputs may be any that keep to these rules, and one draw needn't show every extreme that they name: The cells of the t-th block of 2048 lie in tile t, and cell_node counts the nodes of that tile's 32 rows row by row from its first row.
All inputs are finite; a program needn't handle non-finite values.
Results may differ from a plain program's by a relative error of at most 0.00017.
Values sent between devices are 32-bit elements; how exact they have to be, the bound alone decides.
A program may use at most 128 MiB of HBM per device.

v0:
```python
import jax
import jax.numpy as jnp
from jax import lax
from jax.sharding import PartitionSpec as P

PULSE = 4


def with_halo(cells, sides, width):
    for axis, dim in sides:
        count = lax.axis_size(axis)
        ends = count - 1
        head = lax.slice_in_dim(cells, 0, width, axis=dim)
        tail = lax.slice_in_dim(cells, cells.shape[dim] - width, cells.shape[dim], axis=dim)
        cells = jnp.concatenate(
            [
                lax.ppermute(tail, axis, [(i, (i + 1) % count) for i in range(ends)]),
                cells,
                lax.ppermute(head, axis, [((i + 1) % count, i) for i in range(ends)]),
            ],
            axis=dim,
        )
    return cells


def from_behind(value, axis, steps):
    count = lax.axis_size(axis)
    pairs = [(source, (source + steps) % count) for source in range(count)]
    return lax.ppermute(value, axis, pairs)


def with_edges(voltage):
    return with_halo(voltage, (("tile", 2),), 1)


def currents(
    cell_node, cell_phase, cell_amp, start_sample, sample_count, period, row_count, col_count
):
    sample_ids = start_sample + jnp.arange(sample_count, dtype=jnp.int32)
    delay = jnp.mod(sample_ids[:, None] - cell_phase[None, :], period)
    weights = cell_amp[None, :] * jnp.where(
        delay < PULSE, (PULSE - delay).astype(jnp.float32) / PULSE, 0.0
    )
    injected = (
        jnp.zeros((sample_count, row_count * col_count), jnp.float32).at[:, cell_node].add(weights)
    )
    injected = injected.reshape(sample_count, row_count, col_count)
    return jnp.stack([injected, jnp.zeros_like(injected)])


def residual(extended, history, right_side, coefficients):
    cap_rate, horiz_cond, vert_cond, via_cond = coefficients
    middle = extended[:, :, 1:-1]
    timeline = jnp.concatenate([history, middle], axis=1)
    capacitive = cap_rate[:, None] * (
        1.5 * middle - 2.0 * timeline[:, 1:-1] + 0.5 * timeline[:, :-2]
    )
    padded = jnp.pad(middle, ((0, 0), (0, 0), (0, 0), (1, 1)))
    horiz_flow = horiz_cond[:, None] * (2.0 * middle - padded[..., :-2] - padded[..., 2:])
    vert_flow = vert_cond[:, None] * (2.0 * middle - extended[:, :, :-2] - extended[:, :, 2:])
    via_flow = via_cond[None, None] * (middle - middle[::-1])
    return right_side - (capacitive + horiz_flow + vert_flow + via_flow)


def correct(resid, line_inverse):
    layers, sample_count, row_count, col_count = resid.shape
    pieces = resid.reshape(
        layers, sample_count, row_count, line_inverse.shape[1], line_inverse.shape[2]
    )
    correction = jnp.einsum(
        "ltrbj,lbij->ltrbi", pieces, line_inverse, precision=lax.Precision.HIGHEST
    )
    return correction.reshape(resid.shape)


def on_device(
    start_volt,
    cap_rate,
    horiz_cond,
    vert_cond,
    via_cond,
    line_inverse,
    cell_node,
    cell_phase,
    cell_amp,
):
    samples = start_volt.shape[1]
    row_count = start_volt.shape[2]
    col_count = start_volt.shape[3]
    period = samples * lax.axis_size("slab")
    first_sample = lax.axis_index("slab") * samples
    coefficients = (cap_rate, horiz_cond, vert_cond, via_cond)
    right_side = currents(
        cell_node, cell_phase, cell_amp, first_sample, samples, period, row_count, col_count
    )
    voltage = start_volt
    for sweep_index in range(2):
        extended = with_edges(voltage)
        history = from_behind(voltage[:, samples - 2 :], "slab", 1)
        voltage = voltage + correct(
            residual(extended, history, right_side, coefficients), line_inverse
        )
    return voltage


def solution(mesh):
    in_specs = (
        P(None, "slab", "tile", None),
        P(None, "tile", None),
        P(None, "tile", None),
        P(None, "tile", None),
        P("tile", None),
        P(),
        P("tile"),
        P("tile"),
        P("tile"),
    )
    out_specs = P(None, "slab", "tile", None)
    return jax.shard_map(
        on_device, mesh=mesh, in_specs=in_specs, out_specs=out_specs, check_vma=False
    )
```

profile of v0, /device:TPU:185, one launch (start us, length us, event | category | flops | bytes accessed | tf_op | source)
XLA Modules:
  0.0 114.1 jit_solution(8987372299333797199)
XLA Ops:
  0.0 0.0 copy-start
  0.0 2.5 %slice.58 = f32[2,2,32,2048]{3,2,1,0:T(8,128)} slice(f32[2,8,32,2048]{3,2,1,0:T(8,128)} %param.9), slice={[0:2], [6:8], [0:32], [0:2048]} | slice | bytes 2097152 | tf_op jit(solution)/shard_map/slice | solution.py:99
  2.5 1.4 %collective-permute-start = (f32[2,2,32,2048]{3,2,1,0:T(8,128)}, f32[2,2,32,2048]{3,2,1,0:T(8,128)S(1)}, u32[]{:S(2)}, u32[]{:S(2)}) collective-permute-start(f32[2,2,32,2048]{3,2,1,0:T(8,128)} %slice.58), channel_id=1, source_target_pairs={{0,1},{1,2},{2,3},{3,4},{4,5},{5,6},{6,7},{7,8},{8,9},{9,10},{10,1... | collective-permute-start | bytes 3145736 | tf_op jit(solution)/shard_map/ppermute | solution.py:29
  3.9 2.4 %fusion.68 = (f32[2,8,1,2048]{3,2,1,0:T(1,128)}, f32[2,8,1,2048]{3,2,1,0:T(1,128)}) fusion(f32[2,8,32,2048]{3,2,1,0:T(8,128)} %param.9), kind=kLoop, calls=%fused_computation.93 | loop fusion | bytes 524288 | tf_op jit(solution)/shard_map/slice | solution.py:14
  6.3 4.3 %collective-permute-start.1 = (f32[2,8,1,2048]{3,2,1,0:T(1,128)}, f32[2,8,1,2048]{3,2,1,0:T(1,128)S(1)}, u32[]{:S(2)}, u32[]{:S(2)}) collective-permute-start(f32[2,8,1,2048]{3,2,1,0:T(1,128)} %get-tuple-element.7), channel_id=1, source_target_pairs={{0,16},{16,32},{32,48},{48,64},{64,80},{80,96},{96,112},{112,128},... | collective-permute-start | bytes 393224 | tf_op jit(solution)/shard_map/ppermute | solution.py:17
  10.7 3.3 %collective-permute-start.2 = (f32[2,8,1,2048]{3,2,1,0:T(1,128)}, f32[2,8,1,2048]{3,2,1,0:T(1,128)}, u32[]{:S(2)}, u32[]{:S(2)}) collective-permute-start(f32[2,8,1,2048]{3,2,1,0:T(1,128)} %get-tuple-element.8), channel_id=1, source_target_pairs={{16,0},{32,16},{48,32},{64,48},{80,64},{96,80},{112,96},{128,112},... | collective-permute-start | bytes 393224 | tf_op jit(solution)/shard_map/ppermute | solution.py:19
  14.0 0.7 compare_select_fusion
  14.7 25.0 %scatter_custom_fusion = f32[8,65536]{0,1:T(8,128)} fusion(s32[2048]{0:T(1024)S(1)} %compare_select_fusion, f32[]{:T(128)} %constant.12.clone.1, f32[]{:T(128)} %constant.37.clone.1, s32[]{:T(128)} %constant.36.clone.1, s32[]{:T(128)} %constant.11.clone.1, s32[]{:T(128)} %constant.17.clone.1, s32[]{:T(128)} %constant.13.clone.1, s32[2048]{0:T(1024)} %param.16, ...), kind=kCustom, calls=%fused_computation.1 | custom fusion | flops 311296 | bytes 2117632 | tf_op jit(solution)/shard_map/scatter-add | solution.py:45
  39.7 20.1 %copy.13 = f32[1,8,32,2048]{3,2,1,0:T(8,128)} copy(f32[1,8,32,2048]{1,3,2,0:T(8,128)} %bitcast.35) | data formatting | bytes 4194304 | tf_op jit(solution)/shard_map/stack;reshape | solution.py:48
  59.8 0.0 collective-permute-done
  59.8 1.1 constant_dynamic-update-slice_fusion.1
  60.9 0.0 copy-start.1
  60.9 0.0 copy-start.2
  60.9 0.0 copy-start.3
  60.9 4.8 %constant_dynamic-update-slice_fusion = f32[2,10,32,2048]{3,2,1,0:T(8,128)} fusion(f32[2,10,32,2048]{3,2,1,0:T(8,128)} %constant_dynamic-update-slice_fusion.1, f32[2,8,32,2048]{3,2,1,0:T(8,128)} %param.9), kind=kLoop, calls=%fused_computation.89 | loop fusion | bytes 8388608 | tf_op jit(solution)/shard_map/concatenate | solution.py:54
  65.8 0.0 collective-permute-done.1
  65.8 0.0 collective-permute-done.2
  65.8 0.0 copy-done.1
  65.8 0.0 copy-done.2
  65.8 0.1 copy-done.3
  65.8 8.0 %fusion.14 = f32[2,8,4,16,8,128]{5,4,3,2,1,0:T(8,128)S(1)} fusion(f32[2,8,32,2048]{3,2,1,0:T(8,128)S(1)} %copy-done.1, f32[1,8,32,2048]{3,2,1,0:T(8,128)S(1)} %copy-done.2, f32[2,8,1,2048]{3,2,1,0:T(1,128)} %collective-permute-done.2, f32[2,8,1,2048]{3,2,1,0:T(1,128)S(1)} %collective-permute-done.1, ...), kind=kLoop, calls=%fused_computation.25 | loop fusion | flops 22020096 | bytes 20971520
  73.9 0.0 copy-done
  73.9 4.5 %fusion.39 = f32[2,16,8,4,8,128]{5,4,3,2,1,0:T(8,128)S(1)} fusion(f32[2,8,4,16,8,128]{5,4,3,2,1,0:T(8,128)S(1)} %fusion.14, f32[2,16,128,128]{3,2,1,0:T(8,128)S(1)} %copy-done), kind=kOutput, calls=%fused_computation.59 | convolution fusion | flops 1610612736 | bytes 10485760 | tf_op jit(solution)/shard_map/ltrbj,lbij->ltrbi/dot_general | solution.py:70
  78.4 0.9 bitcast_add_fusion.1
  79.2 0.1 slice.78
  79.3 0.6 collective-permute-start.3
  80.0 0.2 fusion.67
  80.2 3.5 %collective-permute-start.4 = (f32[2,8,1,2048]{3,2,1,0:T(1,128)S(1)}, f32[2,8,1,2048]{3,2,1,0:T(1,128)S(1)}, u32[]{:S(2)}, u32[]{:S(2)}) collective-permute-start(f32[2,8,1,2048]{3,2,1,0:T(1,128)S(1)} %get-tuple-element.5), channel_id=1, source_target_pairs={{0,16},{16,32},{32,48},{48,64},{64,80},{80,96},{96,112},{112,128},... | collective-permute-start | bytes 393224 | tf_op jit(solution)/shard_map/ppermute | solution.py:17
  83.6 4.4 %collective-permute-start.5 = (f32[2,8,1,2048]{3,2,1,0:T(1,128)S(1)}, f32[2,8,1,2048]{3,2,1,0:T(1,128)S(1)}, u32[]{:S(2)}, u32[]{:S(2)}) collective-permute-start(f32[2,8,1,2048]{3,2,1,0:T(1,128)S(1)} %get-tuple-element.6), channel_id=1, source_target_pairs={{16,0},{32,16},{48,32},{64,48},{80,64},{96,80},{112,96},{128,112},... | collective-permute-start | bytes 393224 | tf_op jit(solution)/shard_map/ppermute | solution.py:19
  88.1 9.2 %collective-permute-done.4 = f32[2,8,1,2048]{3,2,1,0:T(1,128)S(1)} collective-permute-done((f32[2,8,1,2048]{3,2,1,0:T(1,128)S(1)}, f32[2,8,1,2048]{3,2,1,0:T(1,128)S(1)}, u32[]{:S(2)}, u32[]{:S(2)}) %collective-permute-start.4) | collective-permute-done | bytes 131104 | tf_op jit(solution)/shard_map/ppermute | solution.py:17
  97.3 2.0 %collective-permute-done.5 = f32[2,8,1,2048]{3,2,1,0:T(1,128)S(1)} collective-permute-done((f32[2,8,1,2048]{3,2,1,0:T(1,128)S(1)}, f32[2,8,1,2048]{3,2,1,0:T(1,128)S(1)}, u32[]{:S(2)}, u32[]{:S(2)}) %collective-permute-start.5) | collective-permute-done | bytes 131104 | tf_op jit(solution)/shard_map/ppermute | solution.py:19
  99.3 0.0 copy-start.4
  99.3 0.7 copy-done.4
  100.0 0.0 collective-permute-done.3
  100.0 6.8 %fusion.15 = f32[2,8,4,16,8,128]{5,4,3,2,1,0:T(8,128)S(1)} fusion(f32[2,8,32,2048]{3,2,1,0:T(8,128)S(1)} %bitcast_add_fusion.1, f32[1,8,32,2048]{3,2,1,0:T(8,128)S(1)} %copy-done.2, f32[2,2,32,2048]{3,2,1,0:T(8,128)} %collective-permute-done.3, f32[2,8,1,2048]{3,2,1,0:T(1,128)} %copy-done.4, f32[2,8,1,2048]{3,2,1,0:T(1,128)S(1)} %collective-permute-done.4, ...), kind=kLoop, calls=%fused_computation.26 | loop fusion | flops 24117248 | bytes 13631488
  106.8 4.5 %fusion.42 = f32[2,16,8,4,8,128]{5,4,3,2,1,0:T(8,128)S(1)} fusion(f32[2,8,4,16,8,128]{5,4,3,2,1,0:T(8,128)S(1)} %fusion.15, f32[2,16,128,128]{3,2,1,0:T(8,128)S(1)} %copy-done), kind=kOutput, calls=%fused_computation.60 | convolution fusion | flops 1610612736 | bytes 10485760 | tf_op jit(solution)/shard_map/ltrbj,lbij->ltrbi/dot_general | solution.py:70
  111.2 2.9 %bitcast_add_fusion = f32[2,8,32,2048]{3,2,1,0:T(8,128)} fusion(f32[2,8,32,2048]{3,2,1,0:T(8,128)S(1)} %bitcast_add_fusion.1, f32[2,16,8,4,8,128]{5,4,3,2,1,0:T(8,128)S(1)} %fusion.42), kind=kLoop, calls=%fused_computation.34 | loop fusion | flops 1048576 | bytes 12582912 | tf_op jit(solution)/shard_map/add | solution.py:100
  (1 shorter events, 0.0 us)
Async XLA Ops:
  0.0 73.9 %copy-start = (f32[2,16,128,128]{3,2,1,0:T(8,128)S(1)}, f32[2,16,128,128]{3,2,1,0:T(8,128)}, u32[]{:S(2)}) copy-start(f32[2,16,128,128]{3,2,1,0:T(8,128)} %param.14) | copy-start | bytes 6291460
  2.5 57.4 %collective-permute-start = (f32[2,2,32,2048]{3,2,1,0:T(8,128)}, f32[2,2,32,2048]{3,2,1,0:T(8,128)S(1)}, u32[]{:S(2)}, u32[]{:S(2)}) collective-permute-start(f32[2,2,32,2048]{3,2,1,0:T(8,128)} %slice.58), channel_id=1, source_target_pairs={{0,1},{1,2},{2,3},{3,4},{4,5},{5,6},{6,7},{7,8},{8,9},{9,10},{10,1... | collective-permute-start | bytes 3145736 | tf_op jit(solution)/shard_map/ppermute | solution.py:29
  6.3 59.4 %collective-permute-start.1 = (f32[2,8,1,2048]{3,2,1,0:T(1,128)}, f32[2,8,1,2048]{3,2,1,0:T(1,128)S(1)}, u32[]{:S(2)}, u32[]{:S(2)}) collective-permute-start(f32[2,8,1,2048]{3,2,1,0:T(1,128)} %get-tuple-element.7), channel_id=1, source_target_pairs={{0,16},{16,32},{32,48},{48,64},{64,80},{80,96},{96,112},{112,128},... | collective-permute-start | bytes 393224 | tf_op jit(solution)/shard_map/ppermute | solution.py:17
  10.7 55.1 %collective-permute-start.2 = (f32[2,8,1,2048]{3,2,1,0:T(1,128)}, f32[2,8,1,2048]{3,2,1,0:T(1,128)}, u32[]{:S(2)}, u32[]{:S(2)}) collective-permute-start(f32[2,8,1,2048]{3,2,1,0:T(1,128)} %get-tuple-element.8), channel_id=1, source_target_pairs={{16,0},{32,16},{48,32},{64,48},{80,64},{96,80},{112,96},{128,112},... | collective-permute-start | bytes 393224 | tf_op jit(solution)/shard_map/ppermute | solution.py:19
  60.9 4.9 %copy-start.1 = (f32[2,8,32,2048]{3,2,1,0:T(8,128)S(1)}, f32[2,8,32,2048]{3,2,1,0:T(8,128)}, u32[]{:S(2)}) copy-start(f32[2,8,32,2048]{3,2,1,0:T(8,128)} %param.9) | copy-start | bytes 12582916
  60.9 4.9 %copy-start.2 = (f32[1,8,32,2048]{3,2,1,0:T(8,128)S(1)}, f32[1,8,32,2048]{3,2,1,0:T(8,128)}, u32[]{:S(2)}) copy-start(f32[1,8,32,2048]{3,2,1,0:T(8,128)} %copy.13) | copy-start | bytes 6291460
  60.9 4.9 %copy-start.3 = (f32[32,2048]{1,0:T(8,128)S(1)}, f32[32,2048]{1,0:T(8,128)}, u32[]{:S(2)}) copy-start(f32[32,2048]{1,0:T(8,128)} %param.13) | copy-start | bytes 786436
  79.3 20.7 %collective-permute-start.3 = (f32[2,2,32,2048]{3,2,1,0:T(8,128)S(1)}, f32[2,2,32,2048]{3,2,1,0:T(8,128)}, u32[]{:S(2)}, u32[]{:S(2)}) collective-permute-start(f32[2,2,32,2048]{3,2,1,0:T(8,128)S(1)} %slice.78), channel_id=1, source_target_pairs={{0,1},{1,2},{2,3},{3,4},{4,5},{5,6},{6,7},{7,8},{8,9},{9,10},{10,1... | collective-permute-start | bytes 3145736 | tf_op jit(solution)/shard_map/ppermute | solution.py:29
  80.2 17.2 %collective-permute-start.4 = (f32[2,8,1,2048]{3,2,1,0:T(1,128)S(1)}, f32[2,8,1,2048]{3,2,1,0:T(1,128)S(1)}, u32[]{:S(2)}, u32[]{:S(2)}) collective-permute-start(f32[2,8,1,2048]{3,2,1,0:T(1,128)S(1)} %get-tuple-element.5), channel_id=1, source_target_pairs={{0,16},{16,32},{32,48},{48,64},{64,80},{80,96},{96,112},{112,128},... | collective-permute-start | bytes 393224 | tf_op jit(solution)/shard_map/ppermute | solution.py:17
  83.6 15.7 %collective-permute-start.5 = (f32[2,8,1,2048]{3,2,1,0:T(1,128)S(1)}, f32[2,8,1,2048]{3,2,1,0:T(1,128)S(1)}, u32[]{:S(2)}, u32[]{:S(2)}) collective-permute-start(f32[2,8,1,2048]{3,2,1,0:T(1,128)S(1)} %get-tuple-element.6), channel_id=1, source_target_pairs={{16,0},{32,16},{48,32},{64,48},{80,64},{96,80},{112,96},{128,112},... | collective-permute-start | bytes 393224 | tf_op jit(solution)/shard_map/ppermute | solution.py:19
  99.3 0.7 copy-start.4
where the time goes:
time: 115 us; the launch traced here: 114 us
  other arithmetic  44.3 us (39%)
  local copies, waits for them, and re-layouts  31.9 us (28%)
  starting transfers between devices  17.7 us (15%)
  waiting for transfers between devices  11.2 us (10%)
  matrix products  8.9 us (8%)
    scatter-add x1, other arithmetic, currents(): jnp.zeros((sample_count, row_count * col_count), jnp.float32)  25 us
    another operation x1, local copies, waits for them, and re-layouts, currents(): return jnp.stack([injected, jnp.zeros_like(injected)])  20.1 us
    unnamed x2, other arithmetic  14.8 us
    ppermute x2, waiting for transfers between devices, with_halo(): lax.ppermute(tail, axis, [(i, (i + 1) % count) for i in range(ends)])  9.25 us
    dot_general x2, matrix products, correct(): jnp.einsum('ltrbj,lbij->ltrbi', pieces, line_inverse, precision=lax.Preci...  8.9 us
    ppermute x2, starting transfers between devices, with_halo(): lax.ppermute(tail, axis, [(i, (i + 1) % count) for i in range(ends)])  7.81 us
    ppermute x2, starting transfers between devices, with_halo(): lax.ppermute(head, axis, [((i + 1) % count, i) for i in range(ends)])  7.78 us
    concatenate x1, local copies, waits for them, and re-layouts, residual(): timeline = jnp.concatenate([history, middle], axis=1)  4.84 us
  transfers between devices with their start and end apart: 6, of which 2 were waited for; matrix products, arithmetic and copies ran while one was open for 48% of the time, Pallas kernels for 0%

commit v1 on v0

v1 whole, which is shorter than its diff:
```python
import functools

import jax
import jax.numpy as jnp
from jax import lax
from jax.experimental import pallas as pl
from jax.experimental.pallas import tpu as pltpu
from jax.sharding import PartitionSpec as P

PULSE = 4
LANES = 128
TOP = 8
MESH_ID = pl.DeviceIdType.MESH
BF = jnp.bfloat16
F32 = jnp.float32


def split(value):
    high = value.astype(BF)
    low = (value - high.astype(F32)).astype(BF)
    return high, low


def body(
    tiles,
    slabs,
    volt_in,
    cap_in,
    horiz_in,
    vert_in,
    via_in,
    inverse_in,
    node_in,
    phase_in,
    amp_in,
    out,
    start,
    first,
    cap,
    horiz,
    vert,
    via,
    diag,
    inverse,
    weights,
    source,
    node,
    phase,
    amp,
    column,
    spread,
    onehot,
    load_sem,
    block_sem,
    send_a,
    recv_a,
    send_b,
    recv_b,
    halo_send,
    halo_recv,
):
    samples, rows, cols = volt_in.shape[1], volt_in.shape[2], volt_in.shape[3]
    blocks = cols // LANES
    cells = node.shape[0] * LANES
    tile, slab = lax.axis_index("tile"), lax.axis_index("slab")
    ahead = (tile, lax.rem(slab + 1, slabs))
    behind = (tile, lax.rem(slab + slabs - 1, slabs))
    above, below = (tile - 1, slab), (tile + 1, slab)
    has_above, has_below = tile > 0, tile < tiles - 1
    body_rows = pl.ds(TOP, rows)

    barrier = pltpu.get_barrier_semaphore()
    pl.semaphore_signal(barrier, inc=1, device_id=ahead, device_id_type=MESH_ID)
    pl.semaphore_signal(barrier, inc=1, device_id=behind, device_id_type=MESH_ID)

    @pl.when(has_above)
    def _():
        pl.semaphore_signal(barrier, inc=1, device_id=above, device_id_type=MESH_ID)

    @pl.when(has_below)
    def _():
        pl.semaphore_signal(barrier, inc=1, device_id=below, device_id_type=MESH_ID)

    small = [
        pltpu.make_async_copy(one, other, load_sem.at[i])
        for i, (one, other) in enumerate(
            [
                (node_in, node),
                (phase_in, phase),
                (amp_in, amp),
                (inverse_in, inverse),
                (cap_in, cap),
                (horiz_in, horiz),
                (vert_in, vert),
                (via_in, via),
            ]
        )
    ]

    def load_block(b):
        return pltpu.make_async_copy(
            volt_in.at[:, :, :, pl.ds(pl.multiple_of(b * LANES, LANES), LANES)],
            start.at[:, pl.ds(2, samples), b + 1, body_rows, :],
            block_sem.at[b],
        )

    for copy in small[:3]:
        copy.start()

    @pl.loop(0, blocks)
    def _(b):
        load_block(b).start()

    for copy in small[3:]:
        copy.start()

    pl.semaphore_wait(barrier, 2 + has_above.astype(jnp.int32) + has_below.astype(jnp.int32))

    def send_start(b):
        return pltpu.make_async_remote_copy(
            src_ref=volt_in.at[
                :, pl.ds(samples - 2, 2), :, pl.ds(pl.multiple_of(b * LANES, LANES), LANES)
            ],
            dst_ref=start.at[:, pl.ds(0, 2), b + 1, body_rows, :],
            send_sem=send_a.at[b],
            recv_sem=recv_a.at[b],
            device_id=ahead,
            device_id_type=MESH_ID,
        )

    def send_first(b):
        return pltpu.make_async_remote_copy(
            src_ref=first.at[:, pl.ds(samples, 2), b + 1, body_rows, :],
            dst_ref=first.at[:, pl.ds(0, 2), b + 1, body_rows, :],
            send_sem=send_b.at[b],
            recv_sem=recv_b.at[b],
            device_id=ahead,
            device_id_type=MESH_ID,
        )

    def halo_copies(volt, low, count, slot):
        def one(row, to, device, sem):
            return pltpu.make_async_remote_copy(
                src_ref=volt.at[:, pl.ds(low + 2, count), pl.ds(1, blocks), pl.ds(row, 1), :],
                dst_ref=volt.at[:, pl.ds(low + 2, count), pl.ds(1, blocks), pl.ds(to, 1), :],
                send_sem=halo_send.at[sem],
                recv_sem=halo_recv.at[sem],
                device_id=device,
                device_id_type=MESH_ID,
            )

        up = one(TOP, TOP + rows, above, 2 * slot)
        down = one(TOP + rows - 1, TOP - 1, below, 2 * slot + 1)
        return up, down

    def send_halo(*what):
        up, down = halo_copies(*what)

        @pl.when(has_above)
        def _():
            up.start()

        @pl.when(has_below)
        def _():
            down.start()

    def wait_halo(*what):
        up, down = halo_copies(*what)

        @pl.when(has_below)
        def _():
            up.wait_recv()

        @pl.when(has_above)
        def _():
            down.wait_recv()

    def wait_halo_sent(*what):
        up, down = halo_copies(*what)

        @pl.when(has_above)
        def _():
            up.wait_send()

        @pl.when(has_below)
        def _():
            down.wait_send()

    @pl.loop(0, blocks)
    def _(b):
        send_start(b).start()

    @pl.loop(0, blocks)
    def _(b):
        load_block(b).wait()

    send_halo(start, 0, samples, 0)

    for volt in (start, first):
        for edge in (0, blocks + 1):
            volt[:, 2:, edge, body_rows, :] = jnp.zeros((2, samples, rows, LANES), F32)

        @pl.when(jnp.logical_not(has_above))
        def _():
            volt[:, 2:, :, pl.ds(TOP - 1, 1), :] = jnp.zeros((2, samples, blocks + 2, 1, LANES), F32)

        @pl.when(jnp.logical_not(has_below))
        def _():
            volt[:, 2:, :, pl.ds(TOP + rows, 1), :] = jnp.zeros(
                (2, samples, blocks + 2, 1, LANES), F32
            )

    for copy in small[:3]:
        copy.wait()
    period = samples * slabs
    moments = slab * samples + lax.broadcasted_iota(jnp.int32, (samples, LANES), 0)
    row_ids = lax.broadcasted_iota(jnp.int32, (rows, LANES), 0)

    @pl.loop(0, cells // LANES)
    def _(k):
        nodes = node[pl.ds(k, 1), :]
        delay = moments - phase[pl.ds(k, 1), :]
        delay = jnp.where(delay < 0, delay + period, delay)
        weight = amp[pl.ds(k, 1), :] * jnp.where(
            delay < PULSE, (PULSE - delay).astype(F32) * (1.0 / PULSE), 0.0
        )
        high = weight.astype(BF).astype(F32)
        low = weight - high
        here = row_ids == lax.div(nodes, cols)
        place = pl.ds(pl.multiple_of(k * LANES, LANES), LANES)
        for s in range(samples):
            for part, value in ((0, high), (1, low)):
                spread[pl.ds((part * samples + s) * rows, rows), place] = jnp.where(
                    here, value[s : s + 1, :], 0.0
                ).astype(BF)
        x = lax.rem(nodes, cols).astype(F32)
        column[place, :] = jnp.broadcast_to(x, (LANES, LANES)).T

    wide = 2 * LANES
    lane_ids = lax.broadcasted_iota(jnp.int32, (1, LANES), 1).astype(F32)

    @pl.loop(0, blocks // 2)
    def _(pair):
        base = (pair * wide).astype(F32)
        for half in range(2):
            ids = lane_ids + (base + half * LANES)
            onehot[:, half * LANES : (half + 1) * LANES] = jnp.where(
                column[...] == ids, 1.0, 0.0
            ).astype(BF)
        total = jnp.dot(spread[...], onehot[...], preferred_element_type=F32)
        total = total[: samples * rows] + total[samples * rows :]
        for half in range(2):
            source[:, pair * 2 + half] = total[:, half * LANES : (half + 1) * LANES].reshape(
                samples, rows, LANES
            )

    for copy in small[3:]:
        copy.wait()

    @pl.loop(0, blocks)
    def _(b):
        for l in range(2):
            high, low = split(inverse[l, b].T)
            both = jnp.concatenate([high, low], axis=1)
            weights[l, b] = jnp.concatenate([both, both], axis=0)

    diag[...] = (1.5 * cap[...] + 2.0 * horiz[...]) + (2.0 * vert[...] + via[...][None])

    lanes = lax.broadcasted_iota(jnp.int32, (16, LANES), 1)
    is_first, is_last = lanes == 0, lanes == LANES - 1

    def sweep_block(volt, b, low, count):
        place = pl.ds(pl.multiple_of(b * LANES, LANES), LANES)
        highs = {}
        for h in range(rows // 16):
            strip = pl.ds(16 * h, 16)
            coef = [
                [ref[l, strip, place] for ref in (cap, horiz, vert, diag)] for l in range(2)
            ]
            via_h = via[strip, place]

            def load(l, s, shift=0, side=0):
                return volt[l, s + 2, b + 1 + side, pl.ds(TOP + 16 * h + shift, 16), :]

            for s in range(low, low + count):
                centre = [load(l, s) for l in range(2)]
                for l in range(2):
                    cap_h, horiz_h, vert_h, diag_h = coef[l]
                    mid = centre[l]
                    left = pltpu.roll(jnp.where(is_last, load(l, s, 0, -1), mid), 1, 1)
                    right = pltpu.roll(jnp.where(is_first, load(l, s, 0, 1), mid), LANES - 1, 1)
                    resid = (
                        cap_h * (2.0 * load(l, s - 1) - 0.5 * load(l, s - 2))
                        + horiz_h * (left + right)
                        + vert_h * (load(l, s, -1) + load(l, s, 1))
                        + (via_h * centre[1 - l] - diag_h * mid)
                    )
                    if l == 0:
                        resid = resid + source[s, b, strip, :]
                    highs[l, s, h] = split(resid)
        new = []
        for l in range(2):
            order = [(s, h) for s in range(low, low + count) for h in range(rows // 16)]
            left_side = jnp.concatenate(
                [
                    jnp.concatenate([highs[l, s, h][part] for s, h in order], axis=0)
                    for part in range(2)
                ],
                axis=1,
            )
            product = jnp.dot(left_side, weights[l, b], preferred_element_type=F32)
            change = (product[:, :LANES] + product[:, LANES:]).reshape(count, rows, LANES)
            new.append(volt[l, pl.ds(low + 2, count), b + 1, body_rows, :] + change)
        return new

    def first_sweep(low, count, unroll, before=None, after=None):
        @pl.loop(0, blocks // unroll)
        def _(i):
            for j in range(unroll):
                b = i * unroll + j
                if before is not None:
                    before(b)
                new = sweep_block(start, b, low, count)
                for l in range(2):
                    first[l, pl.ds(low + 2, count), b + 1, body_rows, :] = new[l]
                if after is not None:
                    after(b)

    def second_sweep(low, count, unroll, before=None):
        @pl.loop(0, blocks // unroll)
        def _(i):
            for j in range(unroll):
                b = i * unroll + j
                if before is not None:
                    before(b)
                new = sweep_block(first, b, low, count)
                place = pl.ds(pl.multiple_of(b * LANES, LANES), LANES)
                for l in range(2):
                    out[l, pl.ds(low, count), :, place] = new[l]

    last, middle = (samples - 2, 2), (2, samples - 4)
    wait_halo(start, 0, samples, 0)
    first_sweep(*last, 1, after=lambda b: send_first(b).start())
    send_halo(first, *last, 1)
    first_sweep(*middle, 1)
    send_halo(first, *middle, 2)
    first_sweep(0, 2, 1, before=lambda b: send_start(b).wait_recv())
    send_halo(first, 0, 2, 3)
    wait_halo(first, *last, 1)
    wait_halo(first, *middle, 2)
    second_sweep(2, samples - 2, 1)
    wait_halo(first, 0, 2, 3)
    second_sweep(0, 2, 1, before=lambda b: send_first(b).wait_recv())

    @pl.loop(0, blocks)
    def _(b):
        send_start(b).wait_send()
        send_first(b).wait_send()

    wait_halo_sent(start, 0, samples, 0)
    wait_halo_sent(first, *last, 1)
    wait_halo_sent(first, *middle, 2)
    wait_halo_sent(first, 0, 2, 3)


def on_device(
    tiles,
    slabs,
    start_volt,
    cap_rate,
    horiz_cond,
    vert_cond,
    via_cond,
    line_inverse,
    cell_node,
    cell_phase,
    cell_amp,
):
    _, samples, rows, cols = start_volt.shape
    blocks = cols // LANES
    cells = cell_node.shape[0]
    grid = (2, samples + 2, blocks + 2, rows + 2 * TOP, LANES)
    dma = pltpu.SemaphoreType.DMA
    chunks = (cells // LANES, LANES)
    return pl.pallas_call(
        functools.partial(body, tiles, slabs),
        out_shape=jax.ShapeDtypeStruct(start_volt.shape, F32),
        in_specs=[pl.BlockSpec(memory_space=pl.ANY)] * 9,
        out_specs=pl.BlockSpec(memory_space=pltpu.VMEM),
        scratch_shapes=[
            pltpu.VMEM(grid, F32),
            pltpu.VMEM(grid, F32),
            pltpu.VMEM(cap_rate.shape, F32),
            pltpu.VMEM(cap_rate.shape, F32),
            pltpu.VMEM(cap_rate.shape, F32),
            pltpu.VMEM(via_cond.shape, F32),
            pltpu.VMEM(cap_rate.shape, F32),
            pltpu.VMEM(line_inverse.shape, F32),
            pltpu.VMEM((2, blocks, 2 * LANES, 2 * LANES), BF),
            pltpu.VMEM((samples, blocks, rows, LANES), F32),
            pltpu.VMEM(chunks, jnp.int32),
            pltpu.VMEM(chunks, jnp.int32),
            pltpu.VMEM(chunks, F32),
            pltpu.VMEM((cells, LANES), F32),
            pltpu.VMEM((2 * samples * rows, cells), BF),
            pltpu.VMEM((cells, 2 * LANES), BF),
            dma((8,)),
            dma((blocks,)),
            dma((blocks,)),
            dma((blocks,)),
            dma((blocks,)),
            dma((blocks,)),
            dma((8,)),
            dma((8,)),
        ],
        compiler_params=pltpu.CompilerParams(
            collective_id=0, has_side_effects=True, vmem_limit_bytes=58 * 1024 * 1024
        ),
    )(
        start_volt,
        cap_rate,
        horiz_cond,
        vert_cond,
        via_cond,
        line_inverse,
        cell_node.reshape(chunks),
        cell_phase.reshape(chunks),
        cell_amp.reshape(chunks),
    )


def solution(mesh):
    in_specs = (
        P(None, "slab", "tile", None),
        P(None, "tile", None),
        P(None, "tile", None),
        P(None, "tile", None),
        P("tile", None),
        P(),
        P("tile"),
        P("tile"),
        P("tile"),
    )
    out_specs = P(None, "slab", "tile", None)
    return jax.shard_map(
        functools.partial(on_device, mesh.shape["tile"], mesh.shape["slab"]),
        mesh=mesh,
        in_specs=in_specs,
        out_specs=out_specs,
        check_vma=False,
    )
```

time: 115 us -> 58.2 us (0.51)
  Pallas kernels: 0 us -> 53.4 us
  other arithmetic: 44.3 us -> 0 us
  local copies, waits for them, and re-layouts: 31.9 us -> 4.7 us
  starting transfers between devices: 17.7 us -> 0 us
  waiting for transfers between devices: 11.2 us -> 0 us
  matrix products: 8.9 us -> 0 us
    pallas_call x0 -> x1, Pallas kernels: none -> 53.4 us  [on_device(): pl.pallas_call(functools.partial(body, tiles, slabs), out_shape=jax.Shape...]
    scatter-add x1 -> x0, other arithmetic: 25 us -> none  [currents(): jnp.zeros((sample_count, row_count * col_count), jnp.float32)]
    another operation x1 -> x0, local copies, waits for them, and re-layouts: 20.1 us -> none  [currents(): return jnp.stack([injected, jnp.zeros_like(injected)])]
    ppermute x6 -> x0, starting transfers between devices: 17.7 us -> none  [the longest x2 7.81 us: with_halo(): lax.ppermute(tail, axis, [(i, (i + 1) % count) for i in range(ends)])]
    unnamed x2 -> x0, other arithmetic: 14.8 us -> none
    ppermute x6 -> x0, waiting for transfers between devices: 11.2 us -> none  [the longest x2 9.25 us: with_halo(): lax.ppermute(tail, axis, [(i, (i + 1) % count) for i in range(ends)])]
    dot_general x2 -> x0, matrix products: 8.9 us -> none  [correct(): jnp.einsum('ltrbj,lbij->ltrbi', pieces, line_inverse, precision=lax.Preci...]
    slice x4 -> x0, local copies, waits for them, and re-layouts: 5.18 us -> none  [the longest x2 2.62 us: with_halo(): lax.slice_in_dim(cells, cells.shape[dim] - width, cells.shape[dim], axis=...]
  transfers between devices with their start and end apart: 6 -> 0, of which waited for: 2 -> 0; matrix products, arithmetic and copies ran while one was open for 48% -> 0% of each run, Pallas kernels for 0% -> 0%
where the time goes in v1:
time: 58.2 us; the launch traced here: 58.1 us
  Pallas kernels  53.4 us (92%)
  local copies, waits for them, and re-layouts  4.7 us (8%)
    pallas_call x1, Pallas kernels, on_device(): pl.pallas_call(functools.partial(body, tiles, slabs), out_shape=jax.Shape...  53.4 us
    unnamed x1, local copies, waits for them, and re-layouts  4.7 us

profile of v1, /device:TPU:185, one launch (start us, length us, event | category | flops | bytes accessed | tf_op | source)
XLA Modules:
  0.0 58.1 jit_solution(6284148639239028338)
XLA Ops:
  0.0 53.4 %shard_map.91 = f32[2,8,32,2048]{3,2,1,0:T(8,128)} custom-call(f32[2,8,32,2048]{3,2,1,0:T(8,128)} %volt_in.1, f32[2,32,2048]{2,1,0:T(8,128)} %cap_in.1, f32[2,32,2048]{2,1,0:T(8,128)} %horiz_in.1, f32[2,32,2048]{2,1,0:T(8,128)} %vert_in.1, f32[32,2048]{1,0:T(8,128)} %via_in.1, f32[2,16,128,128]{3,2,1,0:T(8,128)} %inverse_in.1, s32[16,128]{1,0:T(8,128)} %bitcast.3, ...), custom_call_target="tpu_custom_call" | custom-call | tf_op jit(solution)/shard_map/pallas_call | solution.py:385
  53.4 4.7 %copy.11 = f32[2,8,32,2048]{3,2,1,0:T(8,128)} copy(f32[2,8,32,2048]{3,2,1,0:T(8,128)} %shard_map.91) | data formatting | bytes 8388608

commit v2 on v1

--- a/solution.py
+++ b/solution.py
@@ -49,7 +49,6 @@
     amp,
     column,
     spread,
-    onehot,
     load_sem,
     block_sem,
     send_a,
@@ -58,6 +57,9 @@
     recv_b,
     halo_send,
     halo_recv,
+    relayed,
+    relay_send,
+    relay_recv,
 ):
     samples, rows, cols = volt_in.shape[1], volt_in.shape[2], volt_in.shape[3]
     blocks = cols // LANES
@@ -69,17 +71,28 @@
     has_above, has_below = tile > 0, tile < tiles - 1
     body_rows = pl.ds(TOP, rows)
 
+    half = slabs // 2
+    has_relay = half > 2
+    place = lax.rem(slab, half)
+    is_source, is_relay, is_target = place == half - 1, place == 1, place == 0
+    relay = (tile, slab - (half - 2))
+    relay_source = (tile, slab + (half - 2))
+    relay_target = (tile, lax.rem(slab - 1 + half, slabs))
+    target_relay = (tile, lax.rem(slab + 1 + half, slabs))
+
     barrier = pltpu.get_barrier_semaphore()
-    pl.semaphore_signal(barrier, inc=1, device_id=ahead, device_id_type=MESH_ID)
-    pl.semaphore_signal(barrier, inc=1, device_id=behind, device_id_type=MESH_ID)
-
-    @pl.when(has_above)
-    def _():
-        pl.semaphore_signal(barrier, inc=1, device_id=above, device_id_type=MESH_ID)
-
-    @pl.when(has_below)
-    def _():
-        pl.semaphore_signal(barrier, inc=1, device_id=below, device_id_type=MESH_ID)
+
+    def greet(device):
+        pl.semaphore_signal(barrier, inc=1, device_id=device, device_id_type=MESH_ID)
+
+    greet(behind)
+    pl.when(has_above)(lambda: greet(above))
+    pl.when(has_below)(lambda: greet(below))
+    peers = 1 + has_above.astype(jnp.int32) + has_below.astype(jnp.int32)
+    if has_relay:
+        pl.when(is_relay)(lambda: greet(relay_source))
+        pl.when(is_target)(lambda: greet(target_relay))
+        peers = peers + (is_source | is_relay).astype(jnp.int32)
 
     small = [
         pltpu.make_async_copy(one, other, load_sem.at[i])
@@ -114,29 +127,99 @@
     for copy in small[3:]:
         copy.start()
 
-    pl.semaphore_wait(barrier, 2 + has_above.astype(jnp.int32) + has_below.astype(jnp.int32))
-
-    def send_start(b):
-        return pltpu.make_async_remote_copy(
-            src_ref=volt_in.at[
-                :, pl.ds(samples - 2, 2), :, pl.ds(pl.multiple_of(b * LANES, LANES), LANES)
-            ],
-            dst_ref=start.at[:, pl.ds(0, 2), b + 1, body_rows, :],
-            send_sem=send_a.at[b],
-            recv_sem=recv_a.at[b],
-            device_id=ahead,
-            device_id_type=MESH_ID,
-        )
-
-    def send_first(b):
-        return pltpu.make_async_remote_copy(
-            src_ref=first.at[:, pl.ds(samples, 2), b + 1, body_rows, :],
-            dst_ref=first.at[:, pl.ds(0, 2), b + 1, body_rows, :],
-            send_sem=send_b.at[b],
-            recv_sem=recv_b.at[b],
-            device_id=ahead,
-            device_id_type=MESH_ID,
-        )
+    for volt in (start, first):
+        for edge in (0, blocks + 1):
+            volt[:, 2:, edge, body_rows, :] = jnp.zeros((2, samples, rows, LANES), F32)
+
+        @pl.when(jnp.logical_not(has_above))
+        def _():
+            volt[:, 2:, :, pl.ds(TOP - 1, 1), :] = jnp.zeros((2, samples, blocks + 2, 1, LANES), F32)
+
+        @pl.when(jnp.logical_not(has_below))
+        def _():
+            volt[:, 2:, :, pl.ds(TOP + rows, 1), :] = jnp.zeros(
+                (2, samples, blocks + 2, 1, LANES), F32
+            )
+
+    class Exchange:
+        def __init__(self, volt, leaving, send_sem, recv_sem, number):
+            self.volt, self.leaving, self.number = volt, leaving, number
+            self.send_sem, self.recv_sem = send_sem, recv_sem
+
+        def landing(self, b):
+            return self.volt.at[:, pl.ds(0, 2), b + 1, body_rows, :]
+
+        def direct(self, b):
+            return pltpu.make_async_remote_copy(
+                src_ref=self.leaving(b),
+                dst_ref=self.landing(b),
+                send_sem=self.send_sem.at[b],
+                recv_sem=self.recv_sem.at[b],
+                device_id=ahead,
+                device_id_type=MESH_ID,
+            )
+
+        def to_relay(self, b):
+            slot = self.number * (blocks // 2) + b // 2
+            return pltpu.make_async_remote_copy(
+                src_ref=self.leaving(b),
+                dst_ref=relayed.at[slot],
+                send_sem=self.send_sem.at[b],
+                recv_sem=relay_recv.at[slot],
+                device_id=relay,
+                device_id_type=MESH_ID,
+            )
+
+        def onward(self, b):
+            slot = self.number * (blocks // 2) + b // 2
+            return pltpu.make_async_remote_copy(
+                src_ref=relayed.at[slot],
+                dst_ref=self.landing(b),
+                send_sem=relay_send.at[slot],
+                recv_sem=self.recv_sem.at[b],
+                device_id=relay_target,
+                device_id_type=MESH_ID,
+            )
+
+        def send_pair(self, b):
+            self.direct(b).start()
+            if has_relay:
+                pl.when(is_source)(lambda: self.to_relay(b + 1).start())
+                pl.when(jnp.logical_not(is_source))(lambda: self.direct(b + 1).start())
+            else:
+                self.direct(b + 1).start()
+
+        def wait(self, b):
+            self.direct(b).wait_recv()
+
+        def wait_sent(self, b):
+            self.direct(b).wait_send()
+
+        def forward(self, k):
+            if has_relay:
+
+                @pl.when(is_relay)
+                def _():
+                    b = 2 * k + 1
+                    self.to_relay(b).wait_recv()
+                    self.onward(b).start()
+
+        def wait_forwarded(self, k):
+            if has_relay:
+
+                @pl.when(is_relay)
+                def _():
+                    self.onward(2 * k + 1).wait_send()
+
+    def start_leaving(b):
+        lanes_b = pl.ds(pl.multiple_of(b * LANES, LANES), LANES)
+        return volt_in.at[:, pl.ds(samples - 2, 2), :, lanes_b]
+
+    def first_leaving(b):
+        return first.at[:, pl.ds(samples, 2), b + 1, body_rows, :]
+
+    before_one = Exchange(start, start_leaving, send_a, recv_a, 0)
+    before_two = Exchange(first, first_leaving, send_b, recv_b, 1)
 
     def halo_copies(volt, low, count, slot):
         def one(row, to, device, sem):
@@ -186,29 +269,11 @@
         def _():
             down.wait_send()
 
-    @pl.loop(0, blocks)
-    def _(b):
-        send_start(b).start()
-
-    @pl.loop(0, blocks)
-    def _(b):
-        load_block(b).wait()
-
-    send_halo(start, 0, samples, 0)
-
-    for volt in (start, first):
-        for edge in (0, blocks + 1):
-            volt[:, 2:, edge, body_rows, :] = jnp.zeros((2, samples, rows, LANES), F32)
-
-        @pl.when(jnp.logical_not(has_above))
-        def _():
-            volt[:, 2:, :, pl.ds(TOP - 1, 1), :] = jnp.zeros((2, samples, blocks + 2, 1, LANES), F32)
-
-        @pl.when(jnp.logical_not(has_below))
-        def _():
-            volt[:, 2:, :, pl.ds(TOP + rows, 1), :] = jnp.zeros(
-                (2, samples, blocks + 2, 1, LANES), F32
-            )
+    pl.semaphore_wait(barrier, peers)
+
+    @pl.loop(0, blocks // 2)
+    def _(k):
+        before_one.send_pair(2 * k)
 
     for copy in small[:3]:
         copy.wait()
@@ -239,20 +304,40 @@
     wide = 2 * LANES
     lane_ids = lax.broadcasted_iota(jnp.int32, (1, LANES), 1).astype(F32)
 
-    @pl.loop(0, blocks // 2)
-    def _(pair):
-        base = (pair * wide).astype(F32)
-        for half in range(2):
-            ids = lane_ids + (base + half * LANES)
-            onehot[:, half * LANES : (half + 1) * LANES] = jnp.where(
-                column[...] == ids, 1.0, 0.0
-            ).astype(BF)
-        total = jnp.dot(spread[...], onehot[...], preferred_element_type=F32)
-        total = total[: samples * rows] + total[samples * rows :]
-        for half in range(2):
-            source[:, pair * 2 + half] = total[:, half * LANES : (half + 1) * LANES].reshape(
-                samples, rows, LANES
-            )
+    quads = blocks // 4
+
+    @pl.loop(0, quads)
+    def _(quad):
+        for j in range(2):
+            pair = quad * 2 + j
+            base = (pair * wide).astype(F32)
+            hot = jnp.concatenate(
+                [
+                    jnp.where(column[...] == lane_ids + (base + side * LANES), 1.0, 0.0).astype(BF)
+                    for side in range(2)
+                ],
+                axis=1,
+            )
+            total = jnp.dot(spread[...], hot, preferred_element_type=F32)
+            total = total[: samples * rows] + total[samples * rows :]
+            for side in range(2):
+                source[:, pair * 2 + side] = total[:, side * LANES : (side + 1) * LANES].reshape(
+                    samples, rows, LANES
+                )
+
+        @pl.when(quad == 0)
+        def _():
+            @pl.loop(0, blocks)
+            def _(b):
+                load_block(b).wait()
+
+            send_halo(start, 0, samples, 0)
+
+        @pl.when(quad > 0)
+        def _():
+            before_one.forward(quad - 1)
+
+    before_one.forward(quads - 1)
 
     for copy in small[3:]:
         copy.wait()
@@ -260,9 +345,9 @@
     @pl.loop(0, blocks)
     def _(b):
         for l in range(2):
-            high, low = split(inverse[l, b].T)
-            both = jnp.concatenate([high, low], axis=1)
-            weights[l, b] = jnp.concatenate([both, both], axis=0)
+            high, low = split(inverse[l, b])
+            both = jnp.concatenate([high, low], axis=0)
+            weights[l, b] = jnp.concatenate([both, both], axis=1)
 
     diag[...] = (1.5 * cap[...] + 2.0 * horiz[...]) + (2.0 * vert[...] + via[...][None])
 
@@ -308,54 +393,82 @@
                 ],
                 axis=1,
             )
-            product = jnp.dot(left_side, weights[l, b], preferred_element_type=F32)
+            product = lax.dot_general(
+                left_side, weights[l, b], (((1,), (1,)), ((), ())), preferred_element_type=F32
+            )
             change = (product[:, :LANES] + product[:, LANES:]).reshape(count, rows, LANES)
             new.append(volt[l, pl.ds(low + 2, count), b + 1, body_rows, :] + change)
         return new
 
-    def first_sweep(low, count, unroll, before=None, after=None):
-        @pl.loop(0, blocks // unroll)
+    unroll = 4
+    turns = blocks // unroll
+
+    def sweep(volt, low, count, store, before=None, after=None):
+        @pl.loop(0, turns)
         def _(i):
-            for j in range(unroll):
-                b = i * unroll + j
-                if before is not None:
+            taken = [i * unroll + j for j in range(unroll)]
+            if before is not None:
+                for b in taken:
                     before(b)
-                new = sweep_block(start, b, low, count)
-                for l in range(2):
-                    first[l, pl.ds(low + 2, count), b + 1, body_rows, :] = new[l]
-                if after is not None:
-                    after(b)
-
-    def second_sweep(low, count, unroll, before=None):
-        @pl.loop(0, blocks // unroll)
-        def _(i):
-            for j in range(unroll):
-                b = i * unroll + j
-                if before is not None:
-                    before(b)
-                new = sweep_block(first, b, low, count)
-                place = pl.ds(pl.multiple_of(b * LANES, LANES), LANES)
-                for l in range(2):
-                    out[l, pl.ds(low, count), :, place] = new[l]
-
+            for b in taken:
+                store(b, low, count, sweep_block(volt, b, low, count))
+            if after is not None:
+                after(i)
+
+    def to_first(b, low, count, new):
+        for l in range(2):
+            first[l, pl.ds(low + 2, count), b + 1, body_rows, :] = new[l]
+
+    def to_out(b, low, count, new):
+        lanes_b = pl.ds(pl.multiple_of(b * LANES, LANES), LANES)
+        for l in range(2):
+            out[l, pl.ds(low, count), :, lanes_b] = new[l]
+
+    def send_turn(i):
+        for j in range(0, unroll, 2):
+            before_two.send_pair(i * unroll + j)
+
+    def forwards(exchange, shift, turn):
+        def after(i):
+            pl.when(lax.rem(i, turn) == turn - 1)(
+                lambda: exchange.forward(shift + lax.div(i, turn))
+            )
+
+        return after
+
+    relays = blocks // 2
     last, middle = (samples - 2, 2), (2, samples - 4)
     wait_halo(start, 0, samples, 0)
-    first_sweep(*last, 1, after=lambda b: send_first(b).start())
+    sweep(start, *last, to_first, after=send_turn)
     send_halo(first, *last, 1)
-    first_sweep(*middle, 1)
+    sweep(start, *middle, to_first, after=forwards(before_one, quads, 2))
     send_halo(first, *middle, 2)
-    first_sweep(0, 2, 1, before=lambda b: send_start(b).wait_recv())
+
+    @pl.loop(quads + turns // 2, relays)
+    def _(k):
+        before_one.forward(k)
+
+    sweep(start, 0, 2, to_first, before=before_one.wait)
     send_halo(first, 0, 2, 3)
     wait_halo(first, *last, 1)
     wait_halo(first, *middle, 2)
-    second_sweep(2, samples - 2, 1)
+    sweep(first, 2, samples - 2, to_out, after=forwards(before_two, 0, 1))
     wait_halo(first, 0, 2, 3)
-    second_sweep(0, 2, 1, before=lambda b: send_first(b).wait_recv())
+    sweep(first, 0, 2, to_out, before=before_two.wait)
+
+    @pl.loop(turns, relays)
+    def _(k):
+        before_two.forward(k)
 
     @pl.loop(0, blocks)
     def _(b):
-        send_start(b).wait_send()
-        send_first(b).wait_send()
+        before_one.wait_sent(b)
+        before_two.wait_sent(b)
+
+    @pl.loop(0, relays)
+    def _(k):
+        before_one.wait_forwarded(k)
+        before_two.wait_forwarded(k)
 
     wait_halo_sent(start, 0, samples, 0)
     wait_halo_sent(first, *last, 1)
@@ -384,8 +497,8 @@
     chunks = (cells // LANES, LANES)
     return pl.pallas_call(
         functools.partial(body, tiles, slabs),
-        out_shape=jax.ShapeDtypeStruct(start_volt.shape, F32),
-        in_specs=[pl.BlockSpec(memory_space=pl.ANY)] * 9,
+        out_shape=pltpu.VMEM(start_volt.shape, F32),
+        in_specs=[pl.BlockSpec(memory_space=pltpu.HBM)] * 9,
         out_specs=pl.BlockSpec(memory_space=pltpu.VMEM),
         scratch_shapes=[
             pltpu.VMEM(grid, F32),
@@ -403,7 +516,6 @@
             pltpu.VMEM(chunks, F32),
             pltpu.VMEM((cells, LANES), F32),
             pltpu.VMEM((2 * samples * rows, cells), BF),
-            pltpu.VMEM((cells, 2 * LANES), BF),
             dma((8,)),
             dma((blocks,)),
             dma((blocks,)),
@@ -412,20 +524,28 @@
             dma((blocks,)),
             dma((8,)),
             dma((8,)),
+            pltpu.VMEM((blocks, 2, 2, rows, LANES), F32),
+            dma((blocks,)),
+            dma((blocks,)),
         ],
         compiler_params=pltpu.CompilerParams(
-            collective_id=0, has_side_effects=True, vmem_limit_bytes=58 * 1024 * 1024
+            collective_id=0, has_side_effects=True, vmem_limit_bytes=44 * 1024 * 1024
         ),
     )(
-        start_volt,
-        cap_rate,
-        horiz_cond,
-        vert_cond,
-        via_cond,
-        line_inverse,
-        cell_node.reshape(chunks),
-        cell_phase.reshape(chunks),
-        cell_amp.reshape(chunks),
+        *(
+            pltpu.with_memory_space_constraint(value, pltpu.HBM)
+            for value in (
+                start_volt,
+                cap_rate,
+                horiz_cond,
+                vert_cond,
+                via_cond,
+                line_inverse,
+                cell_node.reshape(chunks),
+                cell_phase.reshape(chunks),
+                cell_amp.reshape(chunks),
+            )
+        )
     )
 
 

time: 58.2 us -> 41 us (0.70)
  Pallas kernels: 53.4 us -> 38.5 us
  local copies, waits for them, and re-layouts: 4.7 us -> 2.02 us
    pallas_call x1, Pallas kernels: 53.4 us -> 38.5 us  [on_device(): pl.pallas_call(functools.partial(body, tiles, slabs), out_shape=pltpu.VME...]
    unnamed x1, local copies, waits for them, and re-layouts: 4.7 us -> 2.02 us
where the time goes in v2:
time: 41 us; the launch traced here: 40.5 us
  Pallas kernels  38.5 us (94%)
  local copies, waits for them, and re-layouts  2.02 us (5%)
    pallas_call x1, Pallas kernels, on_device(): pl.pallas_call(functools.partial(body, tiles, slabs), out_shape=pltpu.VME...  38.5 us
    unnamed x1, local copies, waits for them, and re-layouts  2.02 us

profile of v2, /device:TPU:185, one launch (start us, length us, event | category | flops | bytes accessed | tf_op | source)
XLA Modules:
  0.0 40.5 jit_solution(437342781935913065)
XLA Ops:
  0.0 38.5 %shard_map.91 = f32[2,8,32,2048]{3,2,1,0:T(8,128)S(1)} custom-call(f32[2,8,32,2048]{3,2,1,0:T(8,128)} %volt_in.1, f32[2,32,2048]{2,1,0:T(8,128)} %cap_in.1, f32[2,32,2048]{2,1,0:T(8,128)} %horiz_in.1, f32[2,32,2048]{2,1,0:T(8,128)} %vert_in.1, f32[32,2048]{1,0:T(8,128)} %via_in.1, f32[2,16,128,128]{3,2,1,0:T(8,128)} %inverse_in.1, s32[16,128]{1,0:T(8,128)} %bitcast.3, ...), custom_call_target="tpu_custom_call" | custom-call | tf_op jit(solution)/shard_map/pallas_call | solution.py:498
  38.5 2.0 %copy.11 = f32[2,8,32,2048]{3,2,1,0:T(8,128)} copy(f32[2,8,32,2048]{3,2,1,0:T(8,128)S(1)} %shard_map.91) | data formatting | bytes 8388608

commit v3 on v2

--- a/solution.py
+++ b/solution.py
@@ -71,14 +71,14 @@
     has_above, has_below = tile > 0, tile < tiles - 1
     body_rows = pl.ds(TOP, rows)
 
+    relays = blocks // 2
     half = slabs // 2
-    has_relay = half > 2
+    has_relay = half > 1
     place = lax.rem(slab, half)
-    is_source, is_relay, is_target = place == half - 1, place == 1, place == 0
-    relay = (tile, slab - (half - 2))
-    relay_source = (tile, slab + (half - 2))
-    relay_target = (tile, lax.rem(slab - 1 + half, slabs))
-    target_relay = (tile, lax.rem(slab + 1 + half, slabs))
+    is_source, is_relay = place == half - 1, place == 0
+    relay = (tile, slab - (half - 1))
+    relay_source = (tile, slab + (half - 1))
+    relay_target = (tile, lax.rem(slab + half, slabs))
 
     barrier = pltpu.get_barrier_semaphore()
 
@@ -91,7 +91,7 @@
     peers = 1 + has_above.astype(jnp.int32) + has_below.astype(jnp.int32)
     if has_relay:
         pl.when(is_relay)(lambda: greet(relay_source))
-        pl.when(is_target)(lambda: greet(target_relay))
+        pl.when(is_relay)(lambda: greet(relay_target))
         peers = peers + (is_source | is_relay).astype(jnp.int32)
 
     small = [
@@ -160,7 +160,7 @@
             )
 
         def to_relay(self, b):
-            slot = self.number * (blocks // 2) + b // 2
+            slot = self.number * relays + b
             return pltpu.make_async_remote_copy(
                 src_ref=self.leaving(b),
                 dst_ref=relayed.at[slot],
@@ -171,7 +171,7 @@
             )
 
         def onward(self, b):
-            slot = self.number * (blocks // 2) + b // 2
+            slot = self.number * relays + b
             return pltpu.make_async_remote_copy(
                 src_ref=relayed.at[slot],
                 dst_ref=self.landing(b),
@@ -181,13 +181,13 @@
                 device_id_type=MESH_ID,
             )
 
-        def send_pair(self, b):
-            self.direct(b).start()
+        def send(self, b):
             if has_relay:
-                pl.when(is_source)(lambda: self.to_relay(b + 1).start())
-                pl.when(jnp.logical_not(is_source))(lambda: self.direct(b + 1).start())
+                goes_round = is_source & (b < relays)
+                pl.when(goes_round)(lambda: self.to_relay(b).start())
+                pl.when(jnp.logical_not(goes_round))(lambda: self.direct(b).start())
             else:
-                self.direct(b + 1).start()
+                self.direct(b).start()
 
         def wait(self, b):
             self.direct(b).wait_recv()
@@ -195,21 +195,24 @@
         def wait_sent(self, b):
             self.direct(b).wait_send()
 
-        def forward(self, k):
+        def forward(self, low, high):
             if has_relay:
 
                 @pl.when(is_relay)
                 def _():
-                    b = 2 * k + 1
-                    self.to_relay(b).wait_recv()
-                    self.onward(b).start()
-
-        def wait_forwarded(self, k):
+                    @pl.loop(low, high)
+                    def _(b):
+                        self.to_relay(b).wait_recv()
+                        self.onward(b).start()
+
+        def wait_forwarded(self):
             if has_relay:
 
                 @pl.when(is_relay)
                 def _():
-                    self.onward(2 * k + 1).wait_send()
+                    @pl.loop(0, relays)
+                    def _(b):
+                        self.onward(b).wait_send()
 
     def start_leaving(b):
         lanes_b = pl.ds(pl.multiple_of(b * LANES, LANES), LANES)
@@ -271,9 +274,8 @@
 
     pl.semaphore_wait(barrier, peers)
 
-    @pl.loop(0, blocks // 2)
-    def _(k):
-        before_one.send_pair(2 * k)
+    early = blocks // 4
+    pl.loop(0, early)(before_one.send)
 
     for copy in small[:3]:
         copy.wait()
@@ -332,12 +334,11 @@
                 load_block(b).wait()
 
             send_halo(start, 0, samples, 0)
+            pl.loop(early, blocks)(before_one.send)
 
         @pl.when(quad > 0)
         def _():
-            before_one.forward(quad - 1)
-
-    before_one.forward(quads - 1)
+            before_one.forward(2 * quad - 2, 2 * quad)
 
     for copy in small[3:]:
         copy.wait()
@@ -424,52 +425,42 @@
         for l in range(2):
             out[l, pl.ds(low, count), :, lanes_b] = new[l]
 
-    def send_turn(i):
-        for j in range(0, unroll, 2):
-            before_two.send_pair(i * unroll + j)
-
-    def forwards(exchange, shift, turn):
-        def after(i):
-            pl.when(lax.rem(i, turn) == turn - 1)(
-                lambda: exchange.forward(shift + lax.div(i, turn))
-            )
-
-        return after
-
-    relays = blocks // 2
     last, middle = (samples - 2, 2), (2, samples - 4)
+
+    def send_range(low, high):
+        pl.loop(low, high)(before_two.send)
+
+    def after_middle(i):
+        pl.when(i == 1)(lambda: send_range(2, 4))
+
+    def after_inner(i):
+        pl.when(i < 3)(lambda: before_two.forward(2 + 2 * i, jnp.minimum(4 + 2 * i, relays)))
+
     wait_halo(start, 0, samples, 0)
-    sweep(start, *last, to_first, after=send_turn)
+    sweep(start, *last, to_first)
     send_halo(first, *last, 1)
-    sweep(start, *middle, to_first, after=forwards(before_one, quads, 2))
+    send_range(0, 2)
+    before_one.forward(2 * quads - 2, relays)
+    sweep(start, *middle, to_first, after=after_middle)
     send_halo(first, *middle, 2)
-
-    @pl.loop(quads + turns // 2, relays)
-    def _(k):
-        before_one.forward(k)
-
+    send_range(4, blocks // 2)
     sweep(start, 0, 2, to_first, before=before_one.wait)
     send_halo(first, 0, 2, 3)
+    send_range(blocks // 2, blocks)
+    before_two.forward(0, 2)
     wait_halo(first, *last, 1)
     wait_halo(first, *middle, 2)
-    sweep(first, 2, samples - 2, to_out, after=forwards(before_two, 0, 1))
+    sweep(first, 2, samples - 2, to_out, after=after_inner)
     wait_halo(first, 0, 2, 3)
     sweep(first, 0, 2, to_out, before=before_two.wait)
-
-    @pl.loop(turns, relays)
-    def _(k):
-        before_two.forward(k)
 
     @pl.loop(0, blocks)
     def _(b):
         before_one.wait_sent(b)
         before_two.wait_sent(b)
 
-    @pl.loop(0, relays)
-    def _(k):
-        before_one.wait_forwarded(k)
-        before_two.wait_forwarded(k)
-
+    before_one.wait_forwarded()
+    before_two.wait_forwarded()
     wait_halo_sent(start, 0, samples, 0)
     wait_halo_sent(first, *last, 1)
     wait_halo_sent(first, *middle, 2)

time: 41 us -> 38.4 us (0.937)
  the two profiles are of different devices: /device:TPU:185 before, /device:TPU:32 now
where the time goes in v3:
time: 38.4 us; the launch traced here: 38.2 us
  Pallas kernels  36.2 us (94%)
  local copies, waits for them, and re-layouts  2.02 us (5%)
    pallas_call x1, Pallas kernels, on_device(): pl.pallas_call(functools.partial(body, tiles, slabs), out_shape=pltpu.VME...  36.2 us
    unnamed x1, local copies, waits for them, and re-layouts  2.02 us

profile of v3, /device:TPU:32, one launch (start us, length us, event | category | flops | bytes accessed | tf_op | source)
XLA Modules:
  0.0 38.2 jit_solution(3229032718114449109)
XLA Ops:
  0.0 36.2 %shard_map.91 = f32[2,8,32,2048]{3,2,1,0:T(8,128)S(1)} custom-call(f32[2,8,32,2048]{3,2,1,0:T(8,128)} %volt_in.1, f32[2,32,2048]{2,1,0:T(8,128)} %cap_in.1, f32[2,32,2048]{2,1,0:T(8,128)} %horiz_in.1, f32[2,32,2048]{2,1,0:T(8,128)} %vert_in.1, f32[32,2048]{1,0:T(8,128)} %via_in.1, f32[2,16,128,128]{3,2,1,0:T(8,128)} %inverse_in.1, s32[16,128]{1,0:T(8,128)} %bitcast.3, ...), custom_call_target="tpu_custom_call" | custom-call | tf_op jit(solution)/shard_map/pallas_call | solution.py:489
  36.2 2.0 %copy.11 = f32[2,8,32,2048]{3,2,1,0:T(8,128)} copy(f32[2,8,32,2048]{3,2,1,0:T(8,128)S(1)} %shard_map.91) | data formatting | bytes 8388608

commit v4 on v3

--- a/solution.py
+++ b/solution.py
@@ -274,7 +274,7 @@
 
     pl.semaphore_wait(barrier, peers)
 
-    early = blocks // 4
+    early = jnp.where(is_source, relays, blocks // 4) if has_relay else blocks // 4
     pl.loop(0, early)(before_one.send)
 
     for copy in small[:3]:
@@ -434,7 +434,12 @@
         pl.when(i == 1)(lambda: send_range(2, 4))
 
     def after_inner(i):
-        pl.when(i < 3)(lambda: before_two.forward(2 + 2 * i, jnp.minimum(4 + 2 * i, relays)))
+        pl.when(i < 3)(lambda: before_two.forward(3 + 2 * i, jnp.minimum(5 + 2 * i, relays)))
+
+    def after_zero(i):
+        pl.when(lax.rem(i, 2) == 1)(
+            lambda: before_two.forward(lax.div(i, 2), lax.div(i, 2) + 1)
+        )
 
     wait_halo(start, 0, samples, 0)
     sweep(start, *last, to_first)
@@ -444,10 +449,10 @@
     sweep(start, *middle, to_first, after=after_middle)
     send_halo(first, *middle, 2)
     send_range(4, blocks // 2)
-    sweep(start, 0, 2, to_first, before=before_one.wait)
+    sweep(start, 0, 2, to_first, before=before_one.wait, after=after_zero)
     send_halo(first, 0, 2, 3)
     send_range(blocks // 2, blocks)
-    before_two.forward(0, 2)
+    before_two.forward(2, 3)
     wait_halo(first, *last, 1)
     wait_halo(first, *middle, 2)
     sweep(first, 2, samples - 2, to_out, after=after_inner)

time: 38.4 us -> 37.9 us (0.987)
  the two profiles are of different devices: /device:TPU:32 before, /device:TPU:96 now
where the time goes in v4:
time: 37.9 us; the launch traced here: 37.8 us
  Pallas kernels  35.8 us (94%)
  local copies, waits for them, and re-layouts  2.02 us (5%)
    pallas_call x1, Pallas kernels, on_device(): pl.pallas_call(functools.partial(body, tiles, slabs), out_shape=pltpu.VME...  35.8 us
    unnamed x1, local copies, waits for them, and re-layouts  2.02 us

profile of v4, /device:TPU:96, one launch (start us, length us, event | category | flops | bytes accessed | tf_op | source)
XLA Modules:
  0.0 37.8 jit_solution(14632808653121312656)
XLA Ops:
  0.0 35.8 %shard_map.91 = f32[2,8,32,2048]{3,2,1,0:T(8,128)S(1)} custom-call(f32[2,8,32,2048]{3,2,1,0:T(8,128)} %volt_in.1, f32[2,32,2048]{2,1,0:T(8,128)} %cap_in.1, f32[2,32,2048]{2,1,0:T(8,128)} %horiz_in.1, f32[2,32,2048]{2,1,0:T(8,128)} %vert_in.1, f32[32,2048]{1,0:T(8,128)} %via_in.1, f32[2,16,128,128]{3,2,1,0:T(8,128)} %inverse_in.1, s32[16,128]{1,0:T(8,128)} %bitcast.3, ...), custom_call_target="tpu_custom_call" | custom-call | tf_op jit(solution)/shard_map/pallas_call | solution.py:494
  35.8 2.0 %copy.11 = f32[2,8,32,2048]{3,2,1,0:T(8,128)} copy(f32[2,8,32,2048]{3,2,1,0:T(8,128)S(1)} %shard_map.91) | data formatting | bytes 8388608
